TPU v7x, 32 devices: a whole 2x2x4 slice. The times are simulated.
32 devices in a mesh: grp: 2 (over y), node: 4 (over z), feat: 2 (over x), sub: 2 (over core).
Axes of the slice: x: 2, y: 2, z: 4, core: 2. Of those that a mesh axis runs over, the one named last changes fastest.
Arguments:
- features: bfloat16 [16384, 128], P(('grp', 'node', 'sub'), 'feat'), parts along dimension 0, may hold values from -6 to 6
- adjacency: bfloat16 [128, 8, 128, 128], P(('grp', 'node', 'sub')), parts along dimension 0, may hold values from 0 to 0.099609375
- neighbors: int32 [128, 8], P(('grp', 'node', 'sub')), parts along dimension 0, may hold values from 0 to 63, as said below
- edge_mask: int32 [128, 8], P(('grp', 'node', 'sub')), parts along dimension 0, may hold values 0 or 1
- feature_mask: int32 [16384, 128], P(('grp', 'node', 'sub'), 'feat'), parts along dimension 0, may hold values 0 or 1
- weight: bfloat16 [128, 256], P(None, 'feat'), may hold values from -0.5 to 0.5
- cotangent: bfloat16 [16384, 256], P(('grp', 'node', 'sub'), 'feat'), parts along dimension 0, may hold values from -6 to 6
Outputs:
- hidden: bfloat16 [16384, 256], P(('grp', 'node', 'sub'), 'feat'), parts along dimension 0
- grad_weight: float32 [256, 256], P('grp', 'feat'), parts along dimension 0
- grad_features: bfloat16 [16384, 128], P(('grp', 'node', 'sub'), 'feat'), parts along dimension 0
There are 2 independent parts, one for each index of `grp`. A program takes and returns all parts, laid end to end along the dimension named above; an argument that names none is the same for every part. Nothing has to cross between parts.
Inputs may be any that keep to these rules, and one draw needn't show every extreme that they name: `neighbors`: block c is held by owner device c // 8. Over the 64 entries of one device's row blocks, at most 9 entries name blocks of any one owner device.
All inputs are finite; a program needn't handle non-finite values. No bound on the sum of `edge_mask` or of `feature_mask` on one device may be relied on, other than what follows from the above.
Results may differ from a plain program's by a relative error of at most 0.017.
Values may be sent and summed in bfloat16 or wider, within the bound.
A program may use at most 64 MiB of HBM per device.

v0:
```python
import math

import jax
import jax.numpy as jnp
from jax import lax
from jax.sharding import PartitionSpec as P


def activation(values):
    return jax.nn.gelu(values, approximate=True)


def local(features, adjacency, neighbors, edge_mask, feature_mask, weight, cotangent):
    row_count, col_count = features.shape
    blocks_dev, per_block, block_rows, _ = adjacency.shape
    owners = lax.axis_size(("node", "sub"))
    entries = blocks_dev * per_block
    keep_float = feature_mask.astype(jnp.float32)
    dropped = (features.astype(jnp.float32) * keep_float * 2.0).astype(jnp.bfloat16)
    masked = adjacency * edge_mask.astype(jnp.bfloat16)[:, :, None, None]
    flat_ids = neighbors.reshape(entries)
    gathered = lax.all_gather(dropped, ("node", "sub"), axis=0, tiled=True)
    needed = gathered.reshape(owners * blocks_dev, block_rows, col_count)[flat_ids]
    needed = needed.reshape(blocks_dev, per_block, block_rows, col_count)
    summed = jnp.einsum("bkij,bkjf->bif", masked, needed, preferred_element_type=jnp.float32)
    propagated = summed.reshape(row_count, col_count).astype(jnp.bfloat16)
    panel_rows = lax.all_gather(propagated, "feat", axis=1, tiled=True)
    preact = jnp.dot(panel_rows, weight, preferred_element_type=jnp.float32)
    hidden = activation(preact).astype(jnp.bfloat16)
    _, pullback = jax.vjp(activation, preact)
    grad_pre = pullback(cotangent.astype(jnp.float32))[0].astype(jnp.bfloat16)
    grad_scale = 1.0 / math.sqrt(row_count * owners)
    local_weight = (
        jnp.einsum("nf,nh->fh", panel_rows, grad_pre, preferred_element_type=jnp.float32)
        * grad_scale
    )
    grad_weight = lax.psum(local_weight, ("node", "sub"))
    partial_value = jnp.einsum("nh,fh->nf", grad_pre, weight, preferred_element_type=jnp.float32)
    grad_prop = lax.psum_scatter(
        partial_value.astype(jnp.bfloat16), "feat", scatter_dimension=1, tiled=True
    )
    block_terms = jnp.einsum(
        "bkij,bif->bkjf",
        masked,
        grad_prop.reshape(blocks_dev, block_rows, col_count),
        preferred_element_type=jnp.float32,
    ).astype(jnp.bfloat16)
    flat_terms = block_terms.reshape(entries, block_rows * col_count)
    total_blocks = owners * blocks_dev
    onehot = (flat_ids[None, :] == jnp.arange(total_blocks, dtype=jnp.int32)[:, None]).astype(
        jnp.bfloat16
    )
    spread = jnp.dot(onehot, flat_terms, preferred_element_type=jnp.float32).reshape(
        total_blocks * block_rows, col_count
    )
    grad_dropped = lax.psum_scatter(
        spread.astype(jnp.bfloat16), ("node", "sub"), scatter_dimension=0, tiled=True
    ).astype(jnp.float32)
    grad_features = (grad_dropped * keep_float * 2.0).astype(jnp.bfloat16)
    return (hidden, grad_weight, grad_features)


def solution(mesh):
    in_specs = (
        P(("grp", "node", "sub"), "feat"),
        P(("grp", "node", "sub"), None, None, None),
        P(("grp", "node", "sub"), None),
        P(("grp", "node", "sub"), None),
        P(("grp", "node", "sub"), "feat"),
        P(None, "feat"),
        P(("grp", "node", "sub"), "feat"),
    )
    out_specs = (
        P(("grp", "node", "sub"), "feat"),
        P("grp", "feat"),
        P(("grp", "node", "sub"), "feat"),
    )
    return jax.shard_map(local, mesh=mesh, in_specs=in_specs, out_specs=out_specs, check_vma=False)
```

profile of v0, /device:TPU:0, one launch (start us, length us, event | category | flops | bytes accessed | tf_op | source)
XLA Modules:
  0.0 178.6 jit_solution(11301478819624883136)
XLA Ops:
  7.2 1.1 copy.20
  8.4 1.1 copy.19
  9.5 0.8 multiply_convert_fusion.2
  10.4 0.1 reshape.56
  10.5 31.8 %all-gather.2.cloned.1.call-done = bf16[8192,64]{1,0:T(8,128)(2,1)} async-done(((bf16[1024,64]{1,0:T(8,128)(2,1)}), bf16[8192,64]{1,0:T(8,128)(2,1)}) %all-gather.2.cloned.1.call-update) | async-done | bytes 1048592 | tf_op jit(solution)/shard_map/all_gather | solution.py:22
  42.3 2.0 %copy.22 = bf16[64,128,64]{1,2,0:T(8,128)(2,1)S(1)} copy(bf16[64,128,64]{2,1,0:T(8,128)(2,1)} %bitcast.33) | data formatting | bytes 2097152 | tf_op jit(solution)/shard_map/reshape | solution.py:23
  44.3 0.7 gather_fusion
  45.0 2.5 %fusion.13 = bf16[8,8,8,128]{3,2,1,0:T(8,128)(2,1)S(1)} fusion(bf16[8,8,128,64]{2,3,1,0:T(8,128)(2,1)S(1)} %bitcast.32, bf16[8,8,128,128]{3,2,1,0:T(8,128)(2,1)} %param.8, bf16[8,8]{1,0:T(8,128)(2,1)S(1)} %convert_element_type.46), kind=kOutput, calls=%fused_computation.10 | convolution fusion | flops 135331840 | bytes 3276928 | tf_op jit(solution)/shard_map/bkij,bkjf->bif/dot_general | solution.py:25
  47.6 6.3 %all_gather.7 = bf16[1024,128]{0,1:T(8,128)(2,1)S(1)} all-gather(bf16[1024,64]{0,1:T(8,128)(2,1)S(1)} %bitcast.35), channel_id=1, replica_groups=mesh['grp'=2,'node'=4,'feat'=2,'sub'=2] {'feat'}, dimensions={1}, use_global_device_ids=true | all-gather | bytes 393216 | tf_op jit(solution)/shard_map/all_gather | solution.py:27
  53.9 1.3 fusion.20
  55.3 0.9 convolution_convert_fusion.1
  56.3 11.2 %reduce-scatter.3.cloned.1.call-done = bf16[1024,64]{0,1:T(8,128)(2,1)} async-done(((bf16[1024,128]{0,1:T(8,128)(2,1)}), bf16[1024,64]{0,1:T(8,128)(2,1)}) %reduce-scatter.3.cloned.1.call-update) | async-done | bytes 131088 | tf_op jit(solution)/shard_map/reduce_scatter | solution.py:39
  67.5 0.9 copy.34
  68.5 1.6 fusion.4
  70.0 2.0 %copy.25 = bf16[8,8,128,64]{3,2,1,0:T(8,128)(2,1)S(1)} copy(bf16[8,8,128,64]{2,3,1,0:T(8,128)(2,1)} %fusion.4) | data formatting | bytes 2097152 | tf_op jit(solution)/shard_map/convert_element_type | solution.py:47
  72.1 2.5 %reshape.59 = bf16[64,8192]{1,0:T(8,128)(2,1)} reshape(bf16[8,8,128,64]{3,2,1,0:T(8,128)(2,1)S(1)} %copy.25) | data formatting | bytes 2097152 | tf_op jit(solution)/shard_map/reshape | solution.py:48
  74.5 1.6 convolution_convert_fusion
  76.2 3.3 %convert_element_type.58 = bf16[8192,64]{1,0:T(8,128)(2,1)} reshape(bf16[64,8192]{1,0:T(8,128)(2,1)S(1)} %convolution_convert_fusion) | data formatting | bytes 2097152 | tf_op jit(solution)/shard_map/convert_element_type | solution.py:57
  79.6 0.8 convolution_multiply_fusion
  80.4 35.0 %reduce-scatter.5.cloned.1.call-done = bf16[1024,64]{1,0:T(8,128)(2,1)} async-done(((bf16[8192,64]{1,0:T(8,128)(2,1)}), bf16[1024,64]{1,0:T(8,128)(2,1)}) %reduce-scatter.5.cloned.1.call-update) | async-done | bytes 131088 | tf_op jit(solution)/shard_map/reduce_scatter | solution.py:56
  115.4 1.0 multiply_convert_fusion
  116.5 0.8 copy.26
  117.3 53.4 %all-reduce.2.cloned.1.call-done = f32[128,128]{1,0:T(8,128)} async-done(((f32[128,128]{1,0:T(8,128)}), f32[128,128]{1,0:T(8,128)}) %all-reduce.2.cloned.1.call-update) | async-done | bytes 65552 | tf_op jit(solution)/shard_map/psum | solution.py:37
  170.6 1.5 copy.40
  (23 shorter events, 0.4 us)
Async XLA Ops:
  7.2 46.8 %copy-start = (bf16[128,128]{1,0:T(8,128)(2,1)S(1)}, bf16[128,128]{1,0:T(8,128)(2,1)}, u32[]{:S(2)}) copy-start(bf16[128,128]{1,0:T(8,128)(2,1)} %param.12) | copy-start | bytes 98308
  7.2 3.2 %copy-start.2 = (s32[8,8]{1,0:T(8,128)S(1)}, s32[8,8]{1,0:T(8,128)}, u32[]{:S(2)}) copy-start(s32[8,8]{1,0:T(8,128)} %param.9) | copy-start | bytes 772
  7.2 3.3 %copy-start.3 = (s32[8,8]{1,0:T(8,128)S(1)}, s32[8,8]{1,0:T(8,128)}, u32[]{:S(2)}) copy-start(s32[8,8]{1,0:T(8,128)} %param.10) | copy-start | bytes 772
  7.2 35.1 %all-gather.2.cloned.1.call-start = ((), (), s32[]{:S(2)}) async-start(), calls=%async_computation.2 | async-start | bytes 2359296 | tf_op jit(solution)/shard_map/all_gather | solution.py:22
  10.3 57.2 %reduce-scatter.3.cloned.1.call-start = ((), (), s32[]{:S(2)}) async-start(), calls=%async_computation.4 | async-start | bytes 393216 | tf_op jit(solution)/shard_map/reduce_scatter | solution.py:39
  45.0 8.9 %copy-start.4 = (bf16[1024,128]{1,0:T(8,128)(2,1)S(1)}, bf16[1024,128]{1,0:T(8,128)(2,1)}, u32[]{:S(2)}) copy-start(bf16[1024,128]{1,0:T(8,128)(2,1)} %param.13) | copy-start | bytes 786436
  53.9 14.5 %copy-start.1 = (bf16[8,8,128,128]{3,2,1,0:T(8,128)(2,1)S(1)}, bf16[8,8,128,128]{3,2,1,0:T(8,128)(2,1)}, u32[]{:S(2)}) copy-start(bf16[8,8,128,128]{3,2,1,0:T(8,128)(2,1)} %param.8) | copy-start | bytes 6291460
  56.2 59.2 %reduce-scatter.5.cloned.1.call-start = ((), (), s32[]{:S(2)}) async-start(), calls=%async_computation.5 | async-start | bytes 2359296 | tf_op jit(solution)/shard_map/reduce_scatter | solution.py:56
  79.5 91.1 %all-reduce.2.cloned.1.call-start = ((), (), s32[]{:S(2)}) async-start(), calls=%async_computation.3 | async-start | bytes 131072 | tf_op jit(solution)/shard_map/psum | solution.py:37
Sparse Core Ops, SparseCore 0:
  10.4 31.7 all-gather.1
  56.3 11.1 reduce-scatter.2
  79.6 35.7 reduce-scatter.4
  118.3 52.2 all-reduce.1
where the time goes:
time: 179 us
  waiting for transfers between devices  131 us (73%)
  local copies, waits for them, and re-layouts  16.2 us (9%)
  between operations  13.9 us (8%)
  matrix products  8.85 us (5%)
  blocking collectives  6.31 us (4%)
  other arithmetic  1.85 us (1%)
    psum x1, waiting for transfers between devices, local(): grad_weight = lax.psum(local_weight, ('node', 'sub'))  53.4 us
    reduce_scatter x1, waiting for transfers between devices, local(): lax.psum_scatter(spread.astype(jnp.bfloat16), ('node', 'sub'), scatter_di...  35 us
    all_gather x1, waiting for transfers between devices, local(): gathered = lax.all_gather(dropped, ('node', 'sub'), axis=0, tiled=True)  31.8 us
    reduce_scatter x1, waiting for transfers between devices, local(): lax.psum_scatter(partial_value.astype(jnp.bfloat16), 'feat', scatter_dime...  11.2 us
    all_gather x1, blocking collectives, local(): panel_rows = lax.all_gather(propagated, 'feat', axis=1, tiled=True)  6.31 us
    unnamed x15, local copies, waits for them, and re-layouts  5.43 us
  transfers between devices with their start and end apart: 4, of which 4 were waited for; matrix products, arithmetic and copies ran while one was open for 2% of the time, Pallas kernels for 0%

commit v1 on v0

v1 whole, which is shorter than its diff:
```python
import functools
import math

import jax
import jax.numpy as jnp
from jax import lax
from jax.experimental import pallas as pl
from jax.experimental.pallas import tpu as pltpu
from jax.sharding import PartitionSpec as P

MESH = pl.DeviceIdType.MESH
CUBIC = 0.044715
SLOPE = math.sqrt(2.0 / math.pi)


def dot(a, b, ca, cb):
    return lax.dot_general(a, b, (((ca,), (cb,)), ((), ())), preferred_element_type=jnp.float32)


def kernel(
    chips, feats, blocks, per, cap, scale,
    nbr, keep_edge, slot_entry, slot_weight, slot_keep, block_end,
    feat_hbm, mask_hbm, adj_hbm, weight_hbm, cot_hbm,
    hidden_hbm, gw_hbm, gf_hbm,
    feat, fmask, adj, weight, cot, hid, gfo,
    rows, prop, gown, gsend, grecv, terms, runs,
    sown, soth, score, sup, sdown,
    gw, gw_send, gw_recv, gw_chip, gw_out,
    in_sem, out_sem,
    gu_s, gu_r, gd_s, gd_r, gc_s, gc_r,
    p_s, p_r, q_s, q_r,
    c_s, c_r, u_s, u_r, d_s, d_r,
    w_s, w_r, wz_s, wz_r, wo_s, wo_r,
):
    z = lax.axis_index("node")
    f = lax.axis_index("feat")
    q = lax.axis_index("sub")
    half, size = rows.shape[1], rows.shape[2]
    pairs = blocks // 2
    mid = gw.shape[1]

    def remote(src, dst, ss, rs, **where):
        return pltpu.make_async_remote_copy(
            src_ref=src, dst_ref=dst, send_sem=ss, recv_sem=rs,
            device_id=where, device_id_type=MESH,
        )

    def owner_rows(zz, core):
        return rows.at[pl.ds((zz * 2 + core) * blocks, blocks)]

    loads = [
        pltpu.make_async_copy(feat_hbm, feat, in_sem.at[0]),
        pltpu.make_async_copy(mask_hbm, fmask, in_sem.at[1]),
        pltpu.make_async_copy(adj_hbm, adj, in_sem.at[2]),
        pltpu.make_async_copy(cot_hbm, cot, in_sem.at[3]),
    ] + [
        pltpu.make_async_copy(weight_hbm.at[pl.ds(i * half, half)], weight.at[i], in_sem.at[4 + i])
        for i in range(feats)
    ]
    for copy in loads:
        copy.start()

    barrier = pltpu.get_barrier_semaphore()
    for d in range(1, feats):
        pl.semaphore_signal(
            barrier, inc=1, device_id={"feat": lax.rem(f + d, feats)}, device_id_type=MESH
        )
    pl.semaphore_signal(barrier, inc=1, device_id={"sub": 1 - q}, device_id_type=MESH)
    for d in range(1, chips):
        pl.semaphore_signal(
            barrier, inc=1, device_id={"node": lax.rem(z + d, chips)}, device_id_type=MESH
        )

    loads[0].wait()
    loads[1].wait()
    eye_f = (
        lax.broadcasted_iota(jnp.int32, (half, half), 0)
        == lax.broadcasted_iota(jnp.int32, (half, half), 1)
    ).astype(jnp.float32).astype(jnp.bfloat16)
    eye_n = (
        lax.broadcasted_iota(jnp.int32, (size, size), 0)
        == lax.broadcasted_iota(jnp.int32, (size, size), 1)
    ).astype(jnp.float32).astype(jnp.bfloat16)
    base = (z * 2 + q) * blocks
    for b in range(blocks):
        here = pl.ds(b * size, size)
        x = feat[here, :].astype(jnp.float32) * fmask[here, :].astype(jnp.float32) * 2.0
        rows[base + b] = dot(eye_f, x.astype(jnp.bfloat16), 1, 1).astype(jnp.bfloat16)

    pl.semaphore_wait(barrier, chips + feats - 1)

    def gather_up(zz):
        part = owner_rows(zz, q)
        return remote(part, part, gu_s.at[zz], gu_r.at[zz], node=lax.rem(z + 1, chips))

    def gather_down(zz):
        part = owner_rows(zz, q)
        return remote(part, part, gd_s.at[zz], gd_r.at[zz], node=lax.rem(z + chips - 1, chips))

    def gather_core(zz, core):
        part = owner_rows(zz, core)
        return remote(part, part, gc_s.at[zz], gc_r.at[zz], sub=1 - q)

    pl.when(z < chips - 1)(lambda: gather_up(z).start())
    pl.when(z > 0)(lambda: gather_down(z).start())
    gather_core(z, q).start()
    for d in range(1, chips):

        @pl.when(z - d >= 0)
        def _():
            gather_up(z - d).wait_recv()
            pl.when(z < chips - 1)(lambda: gather_up(z - d).start())
            gather_core(z - d, q).start()

        @pl.when(z + d < chips)
        def _():
            gather_down(z + d).wait_recv()
            pl.when(z > 0)(lambda: gather_down(z + d).start())
            gather_core(z + d, q).start()

    loads[2].wait()
    for zz in range(chips):
        gather_core(zz, 1 - q).wait_recv()

    def blocks_of(b):
        return jnp.concatenate([adj[b, k] for k in range(per)], axis=1)

    def send_prop(c, d):
        part = prop.at[f, pl.ds(2 * c, 2)]
        return remote(part, part, p_s.at[d, c], p_r.at[d, c], feat=lax.rem(f + d, feats))

    def recv_prop(c, d):
        part = prop.at[lax.rem(f + feats - d, feats), pl.ds(2 * c, 2)]
        return remote(part, part, p_s.at[d, c], p_r.at[d, c], feat=lax.rem(f + d, feats))

    for c in range(pairs):
        for b in (2 * c, 2 * c + 1):
            parts = []
            for k in range(per):
                e = b * per + k
                live = keep_edge[e].astype(jnp.float32)
                parts.append((rows[nbr[e]].astype(jnp.float32) * live).astype(jnp.bfloat16))
            prop[f, b] = dot(jnp.concatenate(parts, axis=1), blocks_of(b), 1, 1).astype(
                jnp.bfloat16
            )
        for d in range(1, feats):
            send_prop(c, d).start()

    for copy in loads[3:]:
        copy.wait()
    whole_weight = jnp.concatenate([weight[i] for i in range(feats)], axis=0)

    def send_grad(c, d):
        part = pl.ds(2 * c, 2)
        return remote(
            gsend.at[d, part], grecv.at[d, part], q_s.at[d, c], q_r.at[d, c],
            feat=lax.rem(f + d, feats),
        )

    def store_hidden(c):
        part = pl.ds(2 * c * size, 2 * size)
        return pltpu.make_async_copy(hid.at[part], hidden_hbm.at[part], out_sem.at[c])

    total = jnp.zeros((feats * half, weight.shape[2]), jnp.float32)
    for c in range(pairs):
        for d in range(1, feats):
            recv_prop(c, d).wait_recv()
        for b in (2 * c, 2 * c + 1):
            here = pl.ds(b * size, size)
            full = jnp.concatenate([prop[i, b] for i in range(feats)], axis=0)
            v = dot(full, whole_weight, 0, 0)
            square = v * v
            t = jnp.tanh(SLOPE * v * (1.0 + CUBIC * square))
            hid[here, :] = (0.5 * v * (1.0 + t)).astype(jnp.bfloat16)
            slope = 0.5 * (1.0 + t) + 0.5 * v * (1.0 - t * t) * (
                SLOPE * (1.0 + 3.0 * CUBIC * square)
            )
            gp = (cot[here, :].astype(jnp.float32) * slope).astype(jnp.bfloat16)
            total = total + dot(full, gp, 1, 0)
            gown[b] = dot(weight[f], gp, 1, 1)
            for d in range(1, feats):
                gsend[d, b] = dot(weight[lax.rem(f + d, feats)], gp, 1, 1).astype(jnp.bfloat16)
        for d in range(1, feats):
            send_grad(c, d).start()
        store_hidden(c).start()

    gw[0] = total[:mid]
    gw[1] = total[mid:]
    gw_send[...] = gw[1 - q]
    gw_swap = remote(gw_send, gw_recv, w_s, w_r, sub=1 - q)
    gw_swap.start()

    for c in range(pairs):
        for d in range(1, feats):
            send_grad(c, d).wait_recv()
        for b in (2 * c, 2 * c + 1):
            gsum = gown[b]
            for d in range(1, feats):
                gsum = gsum + grecv[d, b].astype(jnp.float32)
            gprop = gsum.astype(jnp.bfloat16)
            out = dot(gprop, blocks_of(b), 1, 0)
            for k in range(per):
                terms[b * per + k] = out[:, k * size:(k + 1) * size]

    gw_swap.wait_recv()
    gw_chip[z] = (gw[q] + gw_recv[...]).astype(jnp.bfloat16)

    def gw_to(d):
        return remote(
            gw_chip.at[z], gw_chip.at[z], wz_s.at[d], wz_r.at[d], node=lax.rem(z + d, chips)
        )

    def gw_from(d):
        part = gw_chip.at[lax.rem(z + chips - d, chips)]
        return remote(part, part, wz_s.at[d], wz_r.at[d], node=lax.rem(z + d, chips))

    for d in range(1, chips):
        gw_to(d).start()

    runs[cap] = jnp.zeros((half, size), jnp.float32)

    def sum_terms(zz, core, dest):
        owner = zz * 2 + core
        total = None
        for s in range(cap):
            p = owner * cap + s
            term = terms[slot_entry[p]] * slot_weight[p].astype(jnp.float32)
            total = term if s == 0 else total * slot_keep[p].astype(jnp.float32) + term
            runs[s] = total
        for i in range(blocks):
            dest[zz, i] = runs[block_end[owner * blocks + i]].astype(jnp.bfloat16)

    def core_copy(zz):
        return remote(soth.at[zz], score.at[zz], c_s.at[zz], c_r.at[zz], sub=1 - q)

    def up_copy(zz):
        return remote(sown.at[zz], sup.at[zz], u_s.at[zz], u_r.at[zz], node=lax.rem(z + 1, chips))

    def down_copy(zz):
        return remote(
            sown.at[zz], sdown.at[zz], d_s.at[zz], d_r.at[zz], node=lax.rem(z + chips - 1, chips)
        )

    def collect(zz):
        sum_terms(zz, 1 - q, soth)
        core_copy(zz).start()
        sum_terms(zz, q, sown)

    def join(zz, other):
        for i in range(blocks):
            sown[zz, i] = (
                sown[zz, i].astype(jnp.float32) + other[zz, i].astype(jnp.float32)
            ).astype(jnp.bfloat16)

    def forward_up(zz):
        core_copy(zz).wait_recv()
        join(zz, score)

        @pl.when(z > 0)
        def _():
            up_copy(zz).wait_recv()
            join(zz, sup)

        up_copy(zz).start()

    def forward_down(zz):
        core_copy(zz).wait_recv()
        join(zz, score)

        @pl.when(z < chips - 1)
        def _():
            down_copy(zz).wait_recv()
            join(zz, sdown)

        down_copy(zz).start()

    for t in range(chips):
        if t < chips - 1:
            pl.when(chips - 1 - t > z)(lambda: collect(chips - 1 - t))
            pl.when(t < z)(lambda: collect(t))
        if t > 0:
            pl.when(chips - t > z)(lambda: forward_up(chips - t))
            pl.when(t - 1 < z)(lambda: forward_down(t - 1))
    collect(z)

    for d in range(1, chips):
        gw_from(d).wait_recv()
    gw_sum = gw_chip[0].astype(jnp.float32)
    for zz in range(1, chips):
        gw_sum = gw_sum + gw_chip[zz].astype(jnp.float32)
    gw_out[q] = gw_sum * scale
    gw_share = remote(gw_out.at[q], gw_out.at[q], wo_s, wo_r, sub=1 - q)
    gw_share_back = remote(gw_out.at[1 - q], gw_out.at[1 - q], wo_s, wo_r, sub=1 - q)
    gw_share.start()

    core_copy(z).wait_recv()

    @pl.when(z > 0)
    def _():
        up_copy(z).wait_recv()

    @pl.when(z < chips - 1)
    def _():
        down_copy(z).wait_recv()

    has_up = z > 0
    has_down = z < chips - 1

    pl.when(jnp.logical_not(has_up))(lambda: sup.__setitem__(z, jnp.zeros_like(sup[z])))
    pl.when(jnp.logical_not(has_down))(lambda: sdown.__setitem__(z, jnp.zeros_like(sdown[z])))
    for b in range(blocks):
        here = pl.ds(b * size, size)
        grad = (
            sown[z, b].astype(jnp.float32)
            + score[z, b].astype(jnp.float32)
            + sup[z, b].astype(jnp.float32)
            + sdown[z, b].astype(jnp.float32)
        ).astype(jnp.bfloat16)
        back = dot(eye_n, grad, 1, 1)
        gfo[here, :] = (back * fmask[here, :].astype(jnp.float32) * 2.0).astype(jnp.bfloat16)
    gf_store = pltpu.make_async_copy(gfo, gf_hbm, out_sem.at[pairs])
    gf_store.start()
    gw_share_back.wait_recv()
    gw_stores = [
        pltpu.make_async_copy(gw_out.at[i], gw_hbm.at[pl.ds(i * mid, mid)], out_sem.at[pairs + 1 + i])
        for i in range(2)
    ]
    for copy in gw_stores:
        copy.start()

    for zz in range(chips):
        gather_core(zz, q).wait_send()
        core_copy(zz).wait_send()

        @pl.when(jnp.logical_and(zz <= z, z < chips - 1))
        def _():
            gather_up(zz).wait_send()

        @pl.when(jnp.logical_and(zz >= z, z > 0))
        def _():
            gather_down(zz).wait_send()

        pl.when(zz > z)(lambda: up_copy(zz).wait_send())
        pl.when(zz < z)(lambda: down_copy(zz).wait_send())
    for c in range(pairs):
        for d in range(1, feats):
            send_prop(c, d).wait_send()
            send_grad(c, d).wait_send()
        store_hidden(c).wait()
    gw_swap.wait_send()
    for d in range(1, chips):
        gw_to(d).wait_send()
    gw_share.wait_send()
    gf_store.wait()
    for copy in gw_stores:
        copy.wait()


def plan(neighbors, edge_mask, owners, blocks, cap):
    n = neighbors.reshape(-1)
    edge = edge_mask.reshape(-1)
    entries = n.shape[0]
    index = jnp.arange(entries, dtype=jnp.int32)
    owner = n // blocks
    same = owner[:, None] == owner[None, :]
    before = (n[None, :] < n[:, None]) | (
        (n[None, :] == n[:, None]) & (index[None, :] < index[:, None])
    )
    rank = jnp.sum((same & before).astype(jnp.int32), axis=1)
    place = owner * cap + rank
    slots = jnp.arange(owners * cap, dtype=jnp.int32)
    hit = (place[:, None] == slots[None, :]).astype(jnp.int32)
    slot_entry = jnp.sum(hit * index[:, None], axis=0)
    slot_weight = jnp.sum(hit * edge[:, None], axis=0)
    first = jnp.sum((same & (n[None, :] == n[:, None]) & before).astype(jnp.int32), axis=1) == 0
    slot_keep = jnp.sum(hit * (1 - first.astype(jnp.int32))[:, None], axis=0)
    names = jnp.arange(owners * blocks, dtype=jnp.int32)
    equal = jnp.sum((n[:, None] == names[None, :]).astype(jnp.int32), axis=0)
    upto = jnp.sum(
        ((owner[:, None] == (names // blocks)[None, :]) & (n[:, None] <= names[None, :])).astype(
            jnp.int32
        ),
        axis=0,
    )
    block_end = jnp.where(equal > 0, upto - 1, cap)
    return n, edge, slot_entry, slot_weight, slot_keep, block_end


def local(chips, features, adjacency, neighbors, edge_mask, feature_mask, weight, cotangent):
    rows_dev, half = features.shape
    blocks, per, size, _ = adjacency.shape
    owners = 2 * chips
    entries = blocks * per
    cap = entries // owners + 1
    total, hid = weight.shape
    feats = total // half
    mid = total // 2
    pairs = blocks // 2
    tables = plan(neighbors, edge_mask, owners, blocks, cap)
    bf, f32 = jnp.bfloat16, jnp.float32
    smem = pl.BlockSpec(memory_space=pltpu.SMEM)
    any_ = pl.BlockSpec(memory_space=pl.ANY)
    dma = pltpu.SemaphoreType.DMA
    body = functools.partial(
        kernel, chips, feats, blocks, per, cap, 1.0 / math.sqrt(rows_dev * owners)
    )
    return pl.pallas_call(
        body,
        out_shape=(
            jax.ShapeDtypeStruct((rows_dev, hid), bf),
            jax.ShapeDtypeStruct((total, hid), f32),
            jax.ShapeDtypeStruct((rows_dev, half), bf),
        ),
        in_specs=[smem] * 6 + [any_] * 5,
        out_specs=(any_, any_, any_),
        scratch_shapes=[
            pltpu.VMEM((rows_dev, half), bf),
            pltpu.VMEM((rows_dev, half), jnp.int32),
            pltpu.VMEM(adjacency.shape, bf),
            pltpu.VMEM((feats, half, hid), bf),
            pltpu.VMEM((rows_dev, hid), bf),
            pltpu.VMEM((rows_dev, hid), bf),
            pltpu.VMEM((rows_dev, half), bf),
            pltpu.VMEM((owners * blocks, half, size), bf),
            pltpu.VMEM((feats, blocks, half, size), bf),
            pltpu.VMEM((blocks, half, size), f32),
            pltpu.VMEM((feats, blocks, half, size), bf),
            pltpu.VMEM((feats, blocks, half, size), bf),
            pltpu.VMEM((entries, half, size), f32),
            pltpu.VMEM((cap + 1, half, size), f32),
        ]
        + [pltpu.VMEM((chips, blocks, half, size), bf)] * 5
        + [
            pltpu.VMEM((2, mid, hid), f32),
            pltpu.VMEM((mid, hid), f32),
            pltpu.VMEM((mid, hid), f32),
            pltpu.VMEM((chips, mid, hid), bf),
            pltpu.VMEM((2, mid, hid), f32),
            dma((4 + feats,)),
            dma((pairs + 3,)),
        ]
        + [dma((chips,))] * 6
        + [dma((feats, pairs))] * 4
        + [dma((chips,))] * 6
        + [dma, dma, dma((chips,)), dma((chips,)), dma, dma],
        compiler_params=pltpu.CompilerParams(
            collective_id=0, has_side_effects=True, vmem_limit_bytes=48 * 1024 * 1024
        ),
    )(*tables, features, feature_mask, adjacency, weight, cotangent)


def solution(mesh):
    split = ("grp", "node", "sub")
    in_specs = (
        P(split, "feat"),
        P(split, None, None, None),
        P(split, None),
        P(split, None),
        P(split, "feat"),
        P(None, "feat"),
        P(split, "feat"),
    )
    out_specs = (P(split, "feat"), P("grp", "feat"), P(split, "feat"))
    return jax.shard_map(
        functools.partial(local, mesh.shape["node"]),
        mesh=mesh, in_specs=in_specs, out_specs=out_specs, check_vma=False,
    )
```

time: 179 us -> 58.4 us (0.33)
  waiting for transfers between devices: 131 us -> 0 us
  Pallas kernels: 0 us -> 47.9 us
  between operations: 13.9 us -> 0.69 us
  matrix products: 8.85 us -> 0 us
  local copies, waits for them, and re-layouts: 16.2 us -> 9.17 us
  blocking collectives: 6.31 us -> 0 us
    psum x1 -> x0, waiting for transfers between devices: 53.4 us -> none  [local(): grad_weight = lax.psum(local_weight, ('node', 'sub'))]
    pallas_call x0 -> x1, Pallas kernels: none -> 47.9 us  [local(): pl.pallas_call(body, out_shape=(jax.ShapeDtypeStruct((rows_dev, hid), bf)...]
    reduce_scatter x2 -> x0, waiting for transfers between devices: 46.2 us -> none  [the longest x1 35 us: local(): lax.psum_scatter(spread.astype(jnp.bfloat16), ('node', 'sub'), scatter_di...]
    all_gather x1 -> x0, waiting for transfers between devices: 31.8 us -> none  [local(): gathered = lax.all_gather(dropped, ('node', 'sub'), axis=0, tiled=True)]
    dot_general x6 -> x0, matrix products: 8.85 us -> none  [the longest x1 2.54 us: local(): jnp.einsum('bkij,bkjf->bif', masked, needed, preferred_element_type=jnp.f...]
    all_gather x1 -> x0, blocking collectives: 6.31 us -> none  [local(): panel_rows = lax.all_gather(propagated, 'feat', axis=1, tiled=True)]
    convert_element_type x3 -> x0, local copies, waits for them, and re-layouts: 5.35 us -> none  [the longest x1 3.31 us: local(): spread.astype(jnp.bfloat16)]
    reshape x3 -> x2, local copies, waits for them, and re-layouts: 4.56 us -> 1.53 us  [the longest x1 0.77 us: plan(): edge = edge_mask.reshape(-1)]
  transfers between devices with their start and end apart: 4 -> 0, of which waited for: 4 -> 0; matrix products, arithmetic and copies ran while one was open for 2% -> 0% of each run, Pallas kernels for 0% -> 0%
where the time goes in v1:
time: 58.4 us; the launch traced here: 58.1 us
  Pallas kernels  47.9 us (82%)
  local copies, waits for them, and re-layouts  9.17 us (16%)
  between operations  0.69 us (1%)
    pallas_call x1, Pallas kernels, local(): pl.pallas_call(body, out_shape=(jax.ShapeDtypeStruct((rows_dev, hid), bf)...  47.9 us
    unnamed x10, local copies, waits for them, and re-layouts  6.85 us

profile of v1, /device:TPU:0, one launch (start us, length us, event | category | flops | bytes accessed | tf_op | source)
XLA Modules:
  0.0 58.1 jit_solution(18130219737912250784)
XLA Ops:
  0.6 0.8 %reshape.102.nbr = s32[64]{0:T(128)S(1)} reshape(s32[8,8]{1,0:T(8,128)} %param.9) | data formatting | bytes 512 | tf_op jit(solution)/shard_map/reshape | solution.py:360
  1.4 0.8 %reshape.103.keep_edge = s32[64]{0:T(128)S(1)} reshape(s32[8,8]{1,0:T(8,128)} %param.10) | data formatting | bytes 512 | tf_op jit(solution)/shard_map/reshape | solution.py:361
  2.2 0.2 convert_reduce_fusion
  2.4 0.1 select_reduce_fusion
  2.5 1.1 %copy.13.feat_hbm = bf16[1024,64]{1,0:T(8,128)(2,1)S(1)} copy(bf16[1024,64]{0,1:T(8,128)(2,1)} %param.7) | data formatting | bytes 262144 | tf_op args[0]
  3.6 1.1 %copy.14.mask_hbm = s32[1024,64]{1,0:T(8,128)S(1)} copy(s32[1024,64]{0,1:T(8,128)} %param.11) | data formatting | bytes 524288 | tf_op args[4]
  4.7 0.0 copy-start
  4.8 1.6 %copy-done = bf16[8,8,128,128]{3,2,1,0:T(8,128)(2,1)S(1)} copy-done((bf16[8,8,128,128]{3,2,1,0:T(8,128)(2,1)S(1)}, bf16[8,8,128,128]{3,2,1,0:T(8,128)(2,1)}, u32[]{:S(2)}) %copy-start) | copy-done | bytes 2097176
  6.3 0.0 copy-start.1
  6.3 0.9 %copy-done.1 = bf16[1024,128]{1,0:T(8,128)(2,1)S(1)} copy-done((bf16[1024,128]{1,0:T(8,128)(2,1)S(1)}, bf16[1024,128]{1,0:T(8,128)(2,1)}, u32[]{:S(2)}) %copy-start.1) | copy-done | bytes 262168
  7.3 0.0 copy-start.2
  7.3 0.8 %copy-done.2 = bf16[128,128]{1,0:T(8,128)(2,1)S(1)} copy-done((bf16[128,128]{1,0:T(8,128)(2,1)S(1)}, bf16[128,128]{1,0:T(8,128)(2,1)}, u32[]{:S(2)}) %copy-start.2) | copy-done | bytes 32792
  8.1 47.9 %shard_map.94 = (bf16[1024,128]{1,0:T(8,128)(2,1)S(1)}, f32[128,128]{1,0:T(8,128)S(1)}, bf16[1024,64]{1,0:T(8,128)(2,1)S(1)}) custom-call(s32[64]{0:T(128)S(1)} %reshape.102.nbr, s32[64]{0:T(128)S(1)} %reshape.103.keep_edge, s32[72]{0:T(128)S(1)} %get-tuple-element.15.slot_entry, s32[72]{0:T(128)S(1)} %get-tuple-element.14.slot_weight, ...), custom_call_target="tpu_custom_call" | custom-call | tf_op jit(solution)/shard_map/pallas_call | solution.py:407
  55.9 0.8 %copy.15 = bf16[1024,64]{0,1:T(8,128)(2,1)} copy(bf16[1024,64]{1,0:T(8,128)(2,1)S(1)} %get-tuple-element.8) | data formatting | bytes 262144 | tf_op jit(solution)/shard_map/pallas_call | solution.py:407
  56.7 0.7 %copy.18 = bf16[1024,128]{1,0:T(8,128)(2,1)} copy(bf16[1024,128]{1,0:T(8,128)(2,1)S(1)} %get-tuple-element.21) | data formatting | bytes 524288
  57.4 0.6 %copy.19 = f32[128,128]{1,0:T(8,128)} copy(f32[128,128]{1,0:T(8,128)S(1)} %get-tuple-element.22) | data formatting | bytes 131072
  (4 shorter events, 0.0 us)
Async XLA Ops:
  4.7 1.6 %copy-start = (bf16[8,8,128,128]{3,2,1,0:T(8,128)(2,1)S(1)}, bf16[8,8,128,128]{3,2,1,0:T(8,128)(2,1)}, u32[]{:S(2)}) copy-start(bf16[8,8,128,128]{3,2,1,0:T(8,128)(2,1)} %adj_hbm.1) | copy-start | bytes 6291460
  6.3 0.9 %copy-start.1 = (bf16[1024,128]{1,0:T(8,128)(2,1)S(1)}, bf16[1024,128]{1,0:T(8,128)(2,1)}, u32[]{:S(2)}) copy-start(bf16[1024,128]{1,0:T(8,128)(2,1)} %cot_hbm.1) | copy-start | bytes 786436
  7.3 0.8 %copy-start.2 = (bf16[128,128]{1,0:T(8,128)(2,1)S(1)}, bf16[128,128]{1,0:T(8,128)(2,1)}, u32[]{:S(2)}) copy-start(bf16[128,128]{1,0:T(8,128)(2,1)} %weight_hbm.1) | copy-start | bytes 98308

commit v2 on v1

--- a/solution.py
+++ b/solution.py
@@ -19,13 +19,14 @@
 
 def kernel(
     chips, feats, blocks, per, cap, scale,
-    nbr, keep_edge, slot_entry, slot_weight, slot_keep, block_end,
+    nbr, keep_edge,
     feat_hbm, mask_hbm, adj_hbm, weight_hbm, cot_hbm,
     hidden_hbm, gw_hbm, gf_hbm,
     feat, fmask, adj, weight, cot, hid, gfo,
     rows, prop, gown, gsend, grecv, terms, runs,
     sown, soth, score, sup, sdown,
     gw, gw_send, gw_recv, gw_chip, gw_out,
+    column, flags, table, tab, tab_sem,
     in_sem, out_sem,
     gu_s, gu_r, gd_s, gd_r, gc_s, gc_r,
     p_s, p_r, q_s, q_r,
@@ -73,19 +74,11 @@
 
     loads[0].wait()
     loads[1].wait()
-    eye_f = (
-        lax.broadcasted_iota(jnp.int32, (half, half), 0)
-        == lax.broadcasted_iota(jnp.int32, (half, half), 1)
-    ).astype(jnp.float32).astype(jnp.bfloat16)
-    eye_n = (
-        lax.broadcasted_iota(jnp.int32, (size, size), 0)
-        == lax.broadcasted_iota(jnp.int32, (size, size), 1)
-    ).astype(jnp.float32).astype(jnp.bfloat16)
     base = (z * 2 + q) * blocks
     for b in range(blocks):
         here = pl.ds(b * size, size)
-        x = feat[here, :].astype(jnp.float32) * fmask[here, :].astype(jnp.float32) * 2.0
-        rows[base + b] = dot(eye_f, x.astype(jnp.bfloat16), 1, 1).astype(jnp.bfloat16)
+        x = feat[:, here].astype(jnp.float32) * fmask[:, here].astype(jnp.float32) * 2.0
+        rows[base + b] = x.astype(jnp.bfloat16)
 
     pl.semaphore_wait(barrier, chips + feats - 1)
 
@@ -104,6 +97,9 @@
     pl.when(z < chips - 1)(lambda: gather_up(z).start())
     pl.when(z > 0)(lambda: gather_down(z).start())
     gather_core(z, q).start()
+    make_tables(blocks, per, cap, nbr, keep_edge, column, flags, table)
+    tab_copy = pltpu.make_async_copy(table, tab, tab_sem)
+    tab_copy.start()
     for d in range(1, chips):
 
         @pl.when(z - d >= 0)
@@ -119,6 +115,7 @@
             gather_core(z + d, q).start()
 
     loads[2].wait()
+    tab_copy.wait()
     for zz in range(chips):
         gather_core(zz, 1 - q).wait_recv()
 
@@ -137,9 +134,8 @@
         for b in (2 * c, 2 * c + 1):
             parts = []
             for k in range(per):
-                e = b * per + k
-                live = keep_edge[e].astype(jnp.float32)
-                parts.append((rows[nbr[e]].astype(jnp.float32) * live).astype(jnp.bfloat16))
+                live = keep_edge[b, k].astype(jnp.float32)
+                parts.append((rows[nbr[b, k]].astype(jnp.float32) * live).astype(jnp.bfloat16))
             prop[f, b] = dot(jnp.concatenate(parts, axis=1), blocks_of(b), 1, 1).astype(
                 jnp.bfloat16
             )
@@ -224,11 +220,11 @@
         total = None
         for s in range(cap):
             p = owner * cap + s
-            term = terms[slot_entry[p]] * slot_weight[p].astype(jnp.float32)
-            total = term if s == 0 else total * slot_keep[p].astype(jnp.float32) + term
+            term = terms[tab[0, p]] * tab[1, p].astype(jnp.float32)
+            total = term if s == 0 else total * tab[2, p].astype(jnp.float32) + term
             runs[s] = total
         for i in range(blocks):
-            dest[zz, i] = runs[block_end[owner * blocks + i]].astype(jnp.bfloat16)
+            dest[zz, i] = runs[tab[3, owner * blocks + i]].astype(jnp.bfloat16)
 
     def core_copy(zz):
         return remote(soth.at[zz], score.at[zz], c_s.at[zz], c_r.at[zz], sub=1 - q)
@@ -315,9 +311,8 @@
             + score[z, b].astype(jnp.float32)
             + sup[z, b].astype(jnp.float32)
             + sdown[z, b].astype(jnp.float32)
-        ).astype(jnp.bfloat16)
-        back = dot(eye_n, grad, 1, 1)
-        gfo[here, :] = (back * fmask[here, :].astype(jnp.float32) * 2.0).astype(jnp.bfloat16)
+        )
+        gfo[:, here] = (grad * fmask[:, here].astype(jnp.float32) * 2.0).astype(jnp.bfloat16)
     gf_store = pltpu.make_async_copy(gfo, gf_hbm, out_sem.at[pairs])
     gf_store.start()
     gw_share_back.wait_recv()
@@ -356,34 +351,41 @@
         copy.wait()
 
 
-def plan(neighbors, edge_mask, owners, blocks, cap):
-    n = neighbors.reshape(-1)
-    edge = edge_mask.reshape(-1)
-    entries = n.shape[0]
-    index = jnp.arange(entries, dtype=jnp.int32)
-    owner = n // blocks
-    same = owner[:, None] == owner[None, :]
-    before = (n[None, :] < n[:, None]) | (
-        (n[None, :] == n[:, None]) & (index[None, :] < index[:, None])
+def make_tables(blocks, per, cap, nbr, keep_edge, column, flags, table):
+    entries, lanes = column.shape
+    width = table.shape[1]
+    int_ = jnp.int32
+    lane = lax.broadcasted_iota(int_, (1, lanes), 1)
+    row = jnp.full((1, lanes), 1 << 20, int_)
+    for e in range(entries):
+        name = nbr[e // per, e % per]
+        column[e:e + 1, :] = jnp.full((1, lanes), name, int_)
+        flags[e:e + 1, :] = jnp.full((1, lanes), keep_edge[e // per, e % per], int_)
+        row = jnp.where(lane == e, name, row)
+    n = column[...]
+    upper = lax.broadcasted_iota(int_, (entries, lanes), 1) < lax.broadcasted_iota(
+        int_, (entries, lanes), 0
     )
-    rank = jnp.sum((same & before).astype(jnp.int32), axis=1)
+    twin = (n == row) & upper
+    below = (lax.div(n, blocks) == lax.div(row, blocks)) & (row < n)
+    rank = jnp.sum(jnp.where(below | twin, 1, 0), axis=1, keepdims=True)
+    twins = jnp.sum(jnp.where(twin, 1, 0), axis=1, keepdims=True)
+    n = n[:, :1]
+    owner = lax.div(n, blocks)
     place = owner * cap + rank
-    slots = jnp.arange(owners * cap, dtype=jnp.int32)
-    hit = (place[:, None] == slots[None, :]).astype(jnp.int32)
-    slot_entry = jnp.sum(hit * index[:, None], axis=0)
-    slot_weight = jnp.sum(hit * edge[:, None], axis=0)
-    first = jnp.sum((same & (n[None, :] == n[:, None]) & before).astype(jnp.int32), axis=1) == 0
-    slot_keep = jnp.sum(hit * (1 - first.astype(jnp.int32))[:, None], axis=0)
-    names = jnp.arange(owners * blocks, dtype=jnp.int32)
-    equal = jnp.sum((n[:, None] == names[None, :]).astype(jnp.int32), axis=0)
+    slot = lax.broadcasted_iota(int_, (entries, width), 1)
+    index = lax.broadcasted_iota(int_, (entries, width), 0)
+    hit = place == slot
+    entry = jnp.sum(jnp.where(hit, index, 0), axis=0, keepdims=True)
+    table[0:1, :] = jnp.clip(entry, 0, entries - 1)
+    table[1:2, :] = jnp.sum(jnp.where(hit, flags[:, :1], 0), axis=0, keepdims=True)
+    table[2:3, :] = jnp.sum(jnp.where(hit & (twins > 0), 1, 0), axis=0, keepdims=True)
+    equal = jnp.sum(jnp.where(n == slot, 1, 0), axis=0, keepdims=True)
     upto = jnp.sum(
-        ((owner[:, None] == (names // blocks)[None, :]) & (n[:, None] <= names[None, :])).astype(
-            jnp.int32
-        ),
-        axis=0,
+        jnp.where((owner == lax.div(slot, blocks)) & (n <= slot), 1, 0), axis=0, keepdims=True
     )
-    block_end = jnp.where(equal > 0, upto - 1, cap)
-    return n, edge, slot_entry, slot_weight, slot_keep, block_end
+    table[3:4, :] = jnp.where(equal > 0, jnp.clip(upto - 1, 0, cap), cap)
+    table[4:8, :] = jnp.zeros((4, width), int_)
 
 
 def local(chips, features, adjacency, neighbors, edge_mask, feature_mask, weight, cotangent):
@@ -396,31 +398,32 @@
     feats = total // half
     mid = total // 2
     pairs = blocks // 2
-    tables = plan(neighbors, edge_mask, owners, blocks, cap)
+    lanes = -(-entries // 128) * 128
+    width = -(-owners * max(blocks, cap) // 128) * 128
     bf, f32 = jnp.bfloat16, jnp.float32
     smem = pl.BlockSpec(memory_space=pltpu.SMEM)
-    any_ = pl.BlockSpec(memory_space=pl.ANY)
+    any_ = pl.BlockSpec(memory_space=pltpu.HBM)
     dma = pltpu.SemaphoreType.DMA
     body = functools.partial(
         kernel, chips, feats, blocks, per, cap, 1.0 / math.sqrt(rows_dev * owners)
     )
-    return pl.pallas_call(
+    hidden, grad_weight, grad_features = pl.pallas_call(
         body,
         out_shape=(
             jax.ShapeDtypeStruct((rows_dev, hid), bf),
             jax.ShapeDtypeStruct((total, hid), f32),
-            jax.ShapeDtypeStruct((rows_dev, half), bf),
+            jax.ShapeDtypeStruct((half, rows_dev), bf),
         ),
-        in_specs=[smem] * 6 + [any_] * 5,
+        in_specs=[smem] * 2 + [any_] * 5,
         out_specs=(any_, any_, any_),
         scratch_shapes=[
-            pltpu.VMEM((rows_dev, half), bf),
-            pltpu.VMEM((rows_dev, half), jnp.int32),
+            pltpu.VMEM((half, rows_dev), bf),
+            pltpu.VMEM((half, rows_dev), jnp.int32),
             pltpu.VMEM(adjacency.shape, bf),
             pltpu.VMEM((feats, half, hid), bf),
             pltpu.VMEM((rows_dev, hid), bf),
             pltpu.VMEM((rows_dev, hid), bf),
-            pltpu.VMEM((rows_dev, half), bf),
+            pltpu.VMEM((half, rows_dev), bf),
             pltpu.VMEM((owners * blocks, half, size), bf),
             pltpu.VMEM((feats, blocks, half, size), bf),
             pltpu.VMEM((blocks, half, size), f32),
@@ -436,6 +439,11 @@
             pltpu.VMEM((mid, hid), f32),
             pltpu.VMEM((chips, mid, hid), bf),
             pltpu.VMEM((2, mid, hid), f32),
+            pltpu.VMEM((entries, lanes), jnp.int32),
+            pltpu.VMEM((entries, lanes), jnp.int32),
+            pltpu.VMEM((8, width), jnp.int32),
+            pltpu.SMEM((8, width), jnp.int32),
+            dma,
             dma((4 + feats,)),
             dma((pairs + 3,)),
         ]
@@ -444,9 +452,10 @@
         + [dma((chips,))] * 6
         + [dma, dma, dma((chips,)), dma((chips,)), dma, dma],
         compiler_params=pltpu.CompilerParams(
-            collective_id=0, has_side_effects=True, vmem_limit_bytes=48 * 1024 * 1024
+            collective_id=0, has_side_effects=True, vmem_limit_bytes=62 * 1024 * 1024
         ),
-    )(*tables, features, feature_mask, adjacency, weight, cotangent)
+    )(neighbors, edge_mask, features.T, feature_mask.T, adjacency, weight, cotangent)
+    return hidden, grad_weight, grad_features.T
 
 
 def solution(mesh):

time: 58.4 us -> 53.9 us (0.923)
  local copies, waits for them, and re-layouts: 9.17 us -> 4.71 us
    unnamed x10 -> x3, local copies, waits for them, and re-layouts: 6.85 us -> 4.71 us
    reshape x2 -> x0, local copies, waits for them, and re-layouts: 1.53 us -> none  [the longest x1 0.77 us: plan(): edge = edge_mask.reshape(-1)]
    pallas_call x1 -> x0, local copies, waits for them, and re-layouts: 0.79 us -> none  [local(): pl.pallas_call(body, out_shape=(jax.ShapeDtypeStruct((rows_dev, hid), bf)...]
where the time goes in v2:
time: 53.9 us; the launch traced here: 53.6 us
  Pallas kernels  48.3 us (90%)
  local copies, waits for them, and re-layouts  4.71 us (9%)
  between operations  0.64 us (1%)
    pallas_call x1, Pallas kernels, local(): pl.pallas_call(body, out_shape=(jax.ShapeDtypeStruct((rows_dev, hid), bf)...  48.3 us
    unnamed x3, local copies, waits for them, and re-layouts  4.71 us

profile of v2, /device:TPU:0, one launch (start us, length us, event | category | flops | bytes accessed | tf_op | source)
XLA Modules:
  0.0 53.6 jit_solution(8837688459680345961)
XLA Ops:
  0.6 48.3 %shard_map.94 = (bf16[1024,128]{1,0:T(8,128)(2,1)}, f32[128,128]{1,0:T(8,128)}, bf16[64,1024]{1,0:T(8,128)(2,1)}) custom-call(s32[8,8]{1,0:T(8,128)} %nbr.1, s32[8,8]{1,0:T(8,128)} %keep_edge.1, bf16[64,1024]{1,0:T(8,128)(2,1)} %bitcast.4, s32[64,1024]{1,0:T(8,128)} %bitcast.3, bf16[8,8,128,128]{3,2,1,0:T(8,128)(2,1)} %adj_hbm.1, ...), custom_call_target="tpu_custom_call" | custom-call | tf_op jit(solution)/shard_map/pallas_call | solution.py:410
  48.9 1.7 %copy.13 = bf16[1024,128]{1,0:T(8,128)(2,1)} copy(bf16[1024,128]{1,0:T(8,128)(2,1)} %get-tuple-element.12) | data formatting | bytes 524288
  50.6 1.5 %copy.14 = f32[128,128]{1,0:T(8,128)} copy(f32[128,128]{1,0:T(8,128)} %get-tuple-element.13) | data formatting | bytes 131072
  52.1 1.6 %copy.15 = bf16[1024,64]{0,1:T(8,128)(2,1)} copy(bf16[1024,64]{0,1:T(8,128)(2,1)} %bitcast.5) | data formatting | bytes 262144

commit v3 on v2

--- a/solution.py
+++ b/solution.py
@@ -24,13 +24,13 @@
     hidden_hbm, gw_hbm, gf_hbm,
     feat, fmask, adj, weight, cot, hid, gfo,
     rows, prop, gown, gsend, grecv, terms, runs,
-    sown, soth, score, sup, sdown,
+    sown, soth, score, landed,
     gw, gw_send, gw_recv, gw_chip, gw_out,
     column, flags, table, tab, tab_sem,
     in_sem, out_sem,
-    gu_s, gu_r, gd_s, gd_r, gc_s, gc_r,
+    g_s, g_r, gc_s, gc_r,
     p_s, p_r, q_s, q_r,
-    c_s, c_r, u_s, u_r, d_s, d_r,
+    c_s, c_r, r_s, r_r,
     w_s, w_r, wz_s, wz_r, wo_s, wo_r,
 ):
     z = lax.axis_index("node")
@@ -39,6 +39,8 @@
     half, size = rows.shape[1], rows.shape[2]
     pairs = blocks // 2
     mid = gw.shape[1]
+    near = sorted(range(1, chips), key=lambda d: min(d, chips - d))
+    far = near[::-1]
 
     def remote(src, dst, ss, rs, **where):
         return pltpu.make_async_remote_copy(
@@ -82,37 +84,27 @@
 
     pl.semaphore_wait(barrier, chips + feats - 1)
 
-    def gather_up(zz):
-        part = owner_rows(zz, q)
-        return remote(part, part, gu_s.at[zz], gu_r.at[zz], node=lax.rem(z + 1, chips))
-
-    def gather_down(zz):
-        part = owner_rows(zz, q)
-        return remote(part, part, gd_s.at[zz], gd_r.at[zz], node=lax.rem(z + chips - 1, chips))
+    def gather_to(d):
+        part = owner_rows(z, q)
+        return remote(part, part, g_s.at[d], g_r.at[d], node=lax.rem(z + d, chips))
+
+    def gather_from(d):
+        part = owner_rows(lax.rem(z + chips - d, chips), q)
+        return remote(part, part, g_s.at[d], g_r.at[d], node=lax.rem(z + d, chips))
 
     def gather_core(zz, core):
         part = owner_rows(zz, core)
         return remote(part, part, gc_s.at[zz], gc_r.at[zz], sub=1 - q)
 
-    pl.when(z < chips - 1)(lambda: gather_up(z).start())
-    pl.when(z > 0)(lambda: gather_down(z).start())
+    for d in far:
+        gather_to(d).start()
     gather_core(z, q).start()
     make_tables(blocks, per, cap, nbr, keep_edge, column, flags, table)
     tab_copy = pltpu.make_async_copy(table, tab, tab_sem)
     tab_copy.start()
-    for d in range(1, chips):
-
-        @pl.when(z - d >= 0)
-        def _():
-            gather_up(z - d).wait_recv()
-            pl.when(z < chips - 1)(lambda: gather_up(z - d).start())
-            gather_core(z - d, q).start()
-
-        @pl.when(z + d < chips)
-        def _():
-            gather_down(z + d).wait_recv()
-            pl.when(z > 0)(lambda: gather_down(z + d).start())
-            gather_core(z + d, q).start()
+    for d in near:
+        gather_from(d).wait_recv()
+        gather_core(lax.rem(z + chips - d, chips), q).start()
 
     loads[2].wait()
     tab_copy.wait()
@@ -229,12 +221,10 @@
     def core_copy(zz):
         return remote(soth.at[zz], score.at[zz], c_s.at[zz], c_r.at[zz], sub=1 - q)
 
-    def up_copy(zz):
-        return remote(sown.at[zz], sup.at[zz], u_s.at[zz], u_r.at[zz], node=lax.rem(z + 1, chips))
-
-    def down_copy(zz):
+    def part_to(d):
         return remote(
-            sown.at[zz], sdown.at[zz], d_s.at[zz], d_r.at[zz], node=lax.rem(z + chips - 1, chips)
+            sown.at[lax.rem(z + d, chips)], landed.at[d], r_s.at[d], r_r.at[d],
+            node=lax.rem(z + d, chips),
         )
 
     def collect(zz):
@@ -242,42 +232,21 @@
         core_copy(zz).start()
         sum_terms(zz, q, sown)
 
-    def join(zz, other):
+    def pass_on(d):
+        zz = lax.rem(z + d, chips)
+        core_copy(zz).wait_recv()
         for i in range(blocks):
             sown[zz, i] = (
-                sown[zz, i].astype(jnp.float32) + other[zz, i].astype(jnp.float32)
+                sown[zz, i].astype(jnp.float32) + score[zz, i].astype(jnp.float32)
             ).astype(jnp.bfloat16)
-
-    def forward_up(zz):
-        core_copy(zz).wait_recv()
-        join(zz, score)
-
-        @pl.when(z > 0)
-        def _():
-            up_copy(zz).wait_recv()
-            join(zz, sup)
-
-        up_copy(zz).start()
-
-    def forward_down(zz):
-        core_copy(zz).wait_recv()
-        join(zz, score)
-
-        @pl.when(z < chips - 1)
-        def _():
-            down_copy(zz).wait_recv()
-            join(zz, sdown)
-
-        down_copy(zz).start()
-
-    for t in range(chips):
-        if t < chips - 1:
-            pl.when(chips - 1 - t > z)(lambda: collect(chips - 1 - t))
-            pl.when(t < z)(lambda: collect(t))
+        part_to(d).start()
+
+    for t, d in enumerate(far):
+        collect(lax.rem(z + d, chips))
         if t > 0:
-            pl.when(chips - t > z)(lambda: forward_up(chips - t))
-            pl.when(t - 1 < z)(lambda: forward_down(t - 1))
+            pass_on(far[t - 1])
     collect(z)
+    pass_on(far[-1])
 
     for d in range(1, chips):
         gw_from(d).wait_recv()
@@ -291,27 +260,13 @@
 
     core_copy(z).wait_recv()
 
-    @pl.when(z > 0)
-    def _():
-        up_copy(z).wait_recv()
-
-    @pl.when(z < chips - 1)
-    def _():
-        down_copy(z).wait_recv()
-
-    has_up = z > 0
-    has_down = z < chips - 1
-
-    pl.when(jnp.logical_not(has_up))(lambda: sup.__setitem__(z, jnp.zeros_like(sup[z])))
-    pl.when(jnp.logical_not(has_down))(lambda: sdown.__setitem__(z, jnp.zeros_like(sdown[z])))
+    for d in near:
+        part_to(d).wait_recv()
     for b in range(blocks):
         here = pl.ds(b * size, size)
-        grad = (
-            sown[z, b].astype(jnp.float32)
-            + score[z, b].astype(jnp.float32)
-            + sup[z, b].astype(jnp.float32)
-            + sdown[z, b].astype(jnp.float32)
-        )
+        grad = sown[z, b].astype(jnp.float32) + score[z, b].astype(jnp.float32)
+        for d in range(1, chips):
+            grad = grad + landed[d, b].astype(jnp.float32)
         gfo[:, here] = (grad * fmask[:, here].astype(jnp.float32) * 2.0).astype(jnp.bfloat16)
     gf_store = pltpu.make_async_copy(gfo, gf_hbm, out_sem.at[pairs])
     gf_store.start()
@@ -326,17 +281,9 @@
     for zz in range(chips):
         gather_core(zz, q).wait_send()
         core_copy(zz).wait_send()
-
-        @pl.when(jnp.logical_and(zz <= z, z < chips - 1))
-        def _():
-            gather_up(zz).wait_send()
-
-        @pl.when(jnp.logical_and(zz >= z, z > 0))
-        def _():
-            gather_down(zz).wait_send()
-
-        pl.when(zz > z)(lambda: up_copy(zz).wait_send())
-        pl.when(zz < z)(lambda: down_copy(zz).wait_send())
+    for d in range(1, chips):
+        gather_to(d).wait_send()
+        part_to(d).wait_send()
     for c in range(pairs):
         for d in range(1, feats):
             send_prop(c, d).wait_send()
@@ -386,6 +333,17 @@
     )
     table[3:4, :] = jnp.where(equal > 0, jnp.clip(upto - 1, 0, cap), cap)
     table[4:8, :] = jnp.zeros((4, width), int_)
+
+
+def store_results(a, b, c, a_out, b_out, c_out, sem):
+    copies = [
+        pltpu.make_async_copy(src, dst, sem.at[i])
+        for i, (src, dst) in enumerate(((a, a_out), (b, b_out), (c, c_out)))
+    ]
+    for copy in copies:
+        copy.start()
+    for copy in copies:
+        copy.wait()
 
 
 def local(chips, features, adjacency, neighbors, edge_mask, feature_mask, weight, cotangent):
@@ -432,7 +390,7 @@
             pltpu.VMEM((entries, half, size), f32),
             pltpu.VMEM((cap + 1, half, size), f32),
         ]
-        + [pltpu.VMEM((chips, blocks, half, size), bf)] * 5
+        + [pltpu.VMEM((chips, blocks, half, size), bf)] * 4
         + [
             pltpu.VMEM((2, mid, hid), f32),
             pltpu.VMEM((mid, hid), f32),
@@ -447,14 +405,23 @@
             dma((4 + feats,)),
             dma((pairs + 3,)),
         ]
-        + [dma((chips,))] * 6
+        + [dma((chips,))] * 4
         + [dma((feats, pairs))] * 4
-        + [dma((chips,))] * 6
+        + [dma((chips,))] * 4
         + [dma, dma, dma((chips,)), dma((chips,)), dma, dma],
         compiler_params=pltpu.CompilerParams(
             collective_id=0, has_side_effects=True, vmem_limit_bytes=62 * 1024 * 1024
         ),
     )(neighbors, edge_mask, features.T, feature_mask.T, adjacency, weight, cotangent)
+    results = (hidden, grad_weight, grad_features)
+    hidden, grad_weight, grad_features = pl.pallas_call(
+        store_results,
+        out_shape=[jax.ShapeDtypeStruct(r.shape, r.dtype) for r in results],
+        in_specs=[any_] * 3,
+        out_specs=[any_] * 3,
+        scratch_shapes=[dma((3,))],
+        compiler_params=pltpu.CompilerParams(vmem_limit_bytes=62 * 1024 * 1024),
+    )(*results)
     return hidden, grad_weight, grad_features.T
 
 

time: 53.9 us -> 57.4 us (1.065)
  Pallas kernels: 48.3 us -> 55.9 us
  local copies, waits for them, and re-layouts: 4.71 us -> 0 us
    pallas_call x0 -> x1, Pallas kernels: none -> 15 us  [local(): pl.pallas_call(store_results, out_shape=[jax.ShapeDtypeStruct(r.shape, r....]
    pallas_call x1, Pallas kernels: 48.3 us -> 40.9 us  [local(): pl.pallas_call(body, out_shape=(jax.ShapeDtypeStruct((rows_dev, hid), bf)...]
    unnamed x3 -> x0, local copies, waits for them, and re-layouts: 4.71 us -> none
where the time goes in v3:
time: 57.4 us; the launch traced here: 56.6 us
  Pallas kernels  55.9 us (97%)
  between operations  0.64 us (1%)
    pallas_call x1, Pallas kernels, local(): pl.pallas_call(body, out_shape=(jax.ShapeDtypeStruct((rows_dev, hid), bf)...  40.9 us
    pallas_call x1, Pallas kernels, local(): pl.pallas_call(store_results, out_shape=[jax.ShapeDtypeStruct(r.shape, r....  15 us

profile of v3, /device:TPU:0, one launch (start us, length us, event | category | flops | bytes accessed | tf_op | source)
XLA Modules:
  0.0 56.6 jit_solution(11030706988764374300)
XLA Ops:
  0.6 40.9 %shard_map.94 = (bf16[1024,128]{1,0:T(8,128)(2,1)}, f32[128,128]{1,0:T(8,128)}, bf16[64,1024]{1,0:T(8,128)(2,1)}) custom-call(s32[8,8]{1,0:T(8,128)} %nbr.1, s32[8,8]{1,0:T(8,128)} %keep_edge.1, bf16[64,1024]{1,0:T(8,128)(2,1)} %bitcast.4, s32[64,1024]{1,0:T(8,128)} %bitcast.3, bf16[8,8,128,128]{3,2,1,0:T(8,128)(2,1)} %adj_hbm.1, ...), custom_call_target="tpu_custom_call" | custom-call | tf_op jit(solution)/shard_map/pallas_call | solution.py:368
  41.5 15.0 %shard_map.95 = (bf16[1024,128]{1,0:T(8,128)(2,1)}, f32[128,128]{1,0:T(8,128)}, bf16[64,1024]{1,0:T(8,128)(2,1)}) custom-call(bf16[1024,128]{1,0:T(8,128)(2,1)} %get-tuple-element.9.a, f32[128,128]{1,0:T(8,128)} %get-tuple-element.10.b, bf16[64,1024]{1,0:T(8,128)(2,1)} %get-tuple-element.11.c), custom_call_target="tpu_custom_call" | custom-call | tf_op jit(solution)/shard_map/pallas_call | solution.py:417

commit v4 on v3

--- a/solution.py
+++ b/solution.py
@@ -333,17 +333,6 @@
     )
     table[3:4, :] = jnp.where(equal > 0, jnp.clip(upto - 1, 0, cap), cap)
     table[4:8, :] = jnp.zeros((4, width), int_)
-
-
-def store_results(a, b, c, a_out, b_out, c_out, sem):
-    copies = [
-        pltpu.make_async_copy(src, dst, sem.at[i])
-        for i, (src, dst) in enumerate(((a, a_out), (b, b_out), (c, c_out)))
-    ]
-    for copy in copies:
-        copy.start()
-    for copy in copies:
-        copy.wait()
 
 
 def local(chips, features, adjacency, neighbors, edge_mask, feature_mask, weight, cotangent):
@@ -413,15 +402,6 @@
             collective_id=0, has_side_effects=True, vmem_limit_bytes=62 * 1024 * 1024
         ),
     )(neighbors, edge_mask, features.T, feature_mask.T, adjacency, weight, cotangent)
-    results = (hidden, grad_weight, grad_features)
-    hidden, grad_weight, grad_features = pl.pallas_call(
-        store_results,
-        out_shape=[jax.ShapeDtypeStruct(r.shape, r.dtype) for r in results],
-        in_specs=[any_] * 3,
-        out_specs=[any_] * 3,
-        scratch_shapes=[dma((3,))],
-        compiler_params=pltpu.CompilerParams(vmem_limit_bytes=62 * 1024 * 1024),
-    )(*results)
     return hidden, grad_weight, grad_features.T
 
 

time: 57.4 us -> 47.1 us (0.82)
  Pallas kernels: 55.9 us -> 40.9 us
  local copies, waits for them, and re-layouts: 0 us -> 4.71 us
    pallas_call x1 -> x0, Pallas kernels: 15 us -> none  [local(): pl.pallas_call(store_results, out_shape=[jax.ShapeDtypeStruct(r.shape, r....]
    unnamed x0 -> x3, local copies, waits for them, and re-layouts: none -> 4.71 us
where the time goes in v4:
time: 47.1 us; the launch traced here: 46.3 us
  Pallas kernels  40.9 us (87%)
  local copies, waits for them, and re-layouts  4.71 us (10%)
  between operations  0.64 us (1%)
    pallas_call x1, Pallas kernels, local(): pl.pallas_call(body, out_shape=(jax.ShapeDtypeStruct((rows_dev, hid), bf)...  40.9 us
    unnamed x3, local copies, waits for them, and re-layouts  4.71 us

profile of v4, /device:TPU:0, one launch (start us, length us, event | category | flops | bytes accessed | tf_op | source)
XLA Modules:
  0.0 46.3 jit_solution(7467547934623944149)
XLA Ops:
  0.6 40.9 %shard_map.94 = (bf16[1024,128]{1,0:T(8,128)(2,1)}, f32[128,128]{1,0:T(8,128)}, bf16[64,1024]{1,0:T(8,128)(2,1)}) custom-call(s32[8,8]{1,0:T(8,128)} %nbr.1, s32[8,8]{1,0:T(8,128)} %keep_edge.1, bf16[64,1024]{1,0:T(8,128)(2,1)} %bitcast.4, s32[64,1024]{1,0:T(8,128)} %bitcast.3, bf16[8,8,128,128]{3,2,1,0:T(8,128)(2,1)} %adj_hbm.1, ...), custom_call_target="tpu_custom_call" | custom-call | tf_op jit(solution)/shard_map/pallas_call | solution.py:357
  41.6 1.7 %copy.13 = bf16[1024,128]{1,0:T(8,128)(2,1)} copy(bf16[1024,128]{1,0:T(8,128)(2,1)} %get-tuple-element.12) | data formatting | bytes 524288
  43.2 1.5 %copy.14 = f32[128,128]{1,0:T(8,128)} copy(f32[128,128]{1,0:T(8,128)} %get-tuple-element.13) | data formatting | bytes 131072
  44.7 1.6 %copy.15 = bf16[1024,64]{0,1:T(8,128)(2,1)} copy(bf16[1024,64]{0,1:T(8,128)(2,1)} %bitcast.5) | data formatting | bytes 262144
